TPU v7x, 256 devices: a whole 4x4x8 slice. The times are simulated.
256 devices in a mesh: blk: 128 (over z, x_hi, y, core), rep: 2 (over x_lo).
Axes of the slice: x: 4 (x_hi: 2, x_lo: 2; x = x_hi * 2 + x_lo), y: 4, z: 8, core: 2. Of those that a mesh axis runs over, the one named last changes fastest.
Arguments:
- image: bfloat16 [2, 98304, 1152], P('rep', 'blk'), may hold values from -52 to 52
- text: bfloat16 [2, 98304, 1152], P('rep', 'blk'), may hold values from -52 to 52
- log_temp: float32 [1], replicated, may hold values from 1 to 2
- bias: float32 [1], replicated, may hold values from -4 to -2
Outputs:
- loss: float32 [1], replicated
- grad_image: float32 [2, 98304, 1152], P('rep', 'blk')
- grad_text: float32 [2, 98304, 1152], P('rep', 'blk')
- grad_temp: float32 [1], replicated
- grad_bias: float32 [1], replicated
All inputs are finite; a program needn't handle non-finite values.
Results may differ from a plain program's by a relative error of at most 0.0034.
Values may be sent and summed in bfloat16 or wider, within the bound.
No kernel may reach another device: no remote copies, remote signals or barrier semaphores. Data moves between devices by JAX's collectives and lax.ppermute only.
A program may use at most 128 MiB of HBM per device.

v0:
```python
import jax
import jax.numpy as jnp
from jax import lax
from jax.sharding import PartitionSpec as P

SPANS = 3


def shifted(block, axis, distance):
    devices = range(lax.axis_size(axis))
    route = [((i - distance) % len(devices), i) for i in devices]
    return lax.ppermute(block, axis, route)


def unit_rows(raw):
    scale = lax.rsqrt(jnp.sum(raw * raw, axis=-1, keepdims=True) + 1e-06)
    return (raw * scale, scale)


def unit_back(grad, normed, scale):
    return (grad - normed * jnp.sum(normed * grad, axis=-1, keepdims=True)) * scale


def pair_block(left, right, temper, offset_bias, positive):
    raw = lax.dot_general(left, right, (((1,), (1,)), ((), ())), preferred_element_type=jnp.float32)
    logits = temper * raw + offset_bias
    rows = left.shape[0]
    diagonal = lax.broadcasted_iota(jnp.int32, (rows, rows), 0) == lax.broadcasted_iota(
        jnp.int32, (rows, rows), 1
    )
    sign = jnp.where(jnp.logical_and(diagonal, positive), 1.0, -1.0).astype(jnp.float32)
    margin = sign * logits
    total = jnp.sum(jnp.logaddexp(0.0, -margin))
    slope = -sign * jax.nn.sigmoid(-margin)
    return (total, jnp.sum(slope * temper * raw), jnp.sum(slope), slope.astype(jnp.bfloat16))


def body(image, text, log_temp, bias):
    temper = jnp.exp(log_temp[0])
    offset_bias = bias[0]
    spans = SPANS
    unit_image, image_scale = unit_rows(image[0].astype(jnp.float32))
    unit_text, text_scale = unit_rows(text[0].astype(jnp.float32))
    image_low = unit_image.astype(jnp.bfloat16)
    moving = unit_text.astype(jnp.bfloat16)
    rows, width = image_low.shape
    grad_left = jnp.zeros((rows, width), jnp.float32)
    zero = jnp.zeros((), jnp.float32)
    loss_sum, temp_sum, bias_sum = (zero, zero, zero)
    carried = jnp.zeros((rows, width), jnp.float32)
    for offset in range(spans):
        if offset > 0:
            moving = shifted(moving, "blk", 1)
            carried = shifted(carried, "blk", 1)
        total, dtemp, dbias, slope_low = pair_block(
            image_low, moving, temper, offset_bias, offset == 0
        )
        grad_left = grad_left + temper * jnp.dot(
            slope_low, moving, preferred_element_type=jnp.float32
        )
        term = temper * lax.dot_general(
            slope_low, image_low, (((0,), (0,)), ((), ())), preferred_element_type=jnp.float32
        )
        carried = carried + term
        part_loss, part_temp, part_bias = lax.psum((total, dtemp, dbias), ("blk", "rep"))
        loss_sum = loss_sum + part_loss
        temp_sum = temp_sum + part_temp
        bias_sum = bias_sum + part_bias
    text_grad = shifted(carried, "blk", -(spans - 1))
    pairs = float(lax.axis_size("rep") * lax.axis_size("blk") * rows * spans * rows)
    grad_image = unit_back(grad_left, unit_image, image_scale)[None]
    grad_text = unit_back(text_grad, unit_text, text_scale)[None]
    return (
        (loss_sum / pairs).reshape(1),
        grad_image,
        grad_text,
        (temp_sum / pairs).reshape(1),
        (bias_sum / pairs).reshape(1),
    )


def solution(mesh):
    return jax.shard_map(
        body,
        mesh=mesh,
        in_specs=(P("rep", "blk", None), P("rep", "blk", None), P(), P()),
        out_specs=(P(), P("rep", "blk", None), P("rep", "blk", None), P(), P()),
        check_vma=False,
    )
```

profile of v0, /device:TPU:52, one launch (start us, length us, event | category | flops | bytes accessed | tf_op | source)
XLA Modules:
  0.0 322.3 jit_solution(11250965191303202246)
XLA Ops:
  2.4 1.9 fusion.22
  4.3 1.9 fusion.16
  6.2 4.4 %fusion.49 = (f32[]{:T(128)}, f32[]{:T(128)}, f32[]{:T(128)}, f32[768,768]{1,0:T(8,128)S(1)}) fusion(f32[]{:T(128)} %bitcast.81, f32[]{:T(128)} %bitcast, bf16[1,768,1152]{2,1,0:T(8,128)(2,1)S(1)} %copy-done, f32[768]{0:T(1024)S(1)} %add_rsqrt_fusion, bf16[1,768,1152]{2,1,0:T(8,128)(2,1)S(1)} %copy-done.1, f32[768]{0:T(1024)S(1)} %add_rsqrt_fusion.1), kind=kOutput, calls=%fused_computation.65 | convolution fusion | flops 1377239040 | bytes 5904404 | tf_op jit(solution)/shard_map/dot_general | solution.py:25
  10.6 2.0 convolution_multiply_fusion.2
  12.7 0.1 collective-permute-start.2
  12.7 0.4 fusion.4
  13.1 1.6 collective-permute-start
  14.8 57.8 %collective-permute-done = bf16[768,1152]{1,0:T(8,128)(2,1)S(1)} collective-permute-done((bf16[768,1152]{1,0:T(8,128)(2,1)S(1)}, bf16[768,1152]{1,0:T(8,128)(2,1)S(1)}, u32[]{:S(2)}, u32[]{:S(2)}) %collective-permute-start) | collective-permute-done | bytes 1769504 | tf_op jit(solution)/shard_map/ppermute | solution.py:12
  72.6 4.2 %fusion.47 = (f32[]{:T(128)}, f32[]{:T(128)}, f32[]{:T(128)}, f32[768,768]{1,0:T(8,128)S(1)}) fusion(f32[]{:T(128)} %bitcast.85, f32[]{:T(128)} %bitcast, bf16[768,1152]{1,0:T(8,128)(2,1)S(1)} %collective-permute-done, bf16[1,768,1152]{2,1,0:T(8,128)(2,1)S(1)} %copy-done.1, f32[768]{0:T(1024)S(1)} %add_rsqrt_fusion.1), kind=kOutput, calls=%fused_computation.64 | convolution fusion | flops 1372225536 | bytes 5901332 | tf_op jit(solution)/shard_map/dot_general | solution.py:25
  76.9 2.0 fusion.10
  78.9 0.1 collective-permute-start.3
  79.0 1.4 collective-permute-start.1
  80.3 58.5 %collective-permute-done.1 = bf16[768,1152]{1,0:T(8,128)(2,1)S(1)} collective-permute-done((bf16[768,1152]{1,0:T(8,128)(2,1)S(1)}, bf16[768,1152]{1,0:T(8,128)(2,1)S(1)}, u32[]{:S(2)}, u32[]{:S(2)}) %collective-permute-start.1) | collective-permute-done | bytes 1769504 | tf_op jit(solution)/shard_map/ppermute | solution.py:12
  138.8 4.3 %fusion.46 = (f32[]{:T(128)}, f32[]{:T(128)}, f32[]{:T(128)}, f32[768,768]{1,0:T(8,128)S(1)}) fusion(f32[]{:T(128)} %bitcast.84, f32[]{:T(128)} %bitcast, bf16[768,1152]{1,0:T(8,128)(2,1)S(1)} %collective-permute-done.1, bf16[1,768,1152]{2,1,0:T(8,128)(2,1)S(1)} %copy-done.1, f32[768]{0:T(1024)S(1)} %add_rsqrt_fusion.1), kind=kOutput, calls=%fused_computation.63 | convolution fusion | flops 1372225536 | bytes 5901332 | tf_op jit(solution)/shard_map/dot_general | solution.py:25
  143.1 1.9 convolution_multiply_fusion
  145.1 2.1 add.113
  147.2 0.4 collective-permute-start.4
  147.6 3.8 %fusion.37 = f32[768,1152]{1,0:T(8,128)} fusion(bf16[768,1152]{1,0:T(8,128)(2,1)S(1)} %fusion.4, f32[768,768]{1,0:T(8,128)S(1)} %get-tuple-element.17, f32[]{:T(128)} %bitcast.78, f32[]{:T(128)} %bitcast), kind=kOutput, calls=%fused_computation.57 | convolution fusion | flops 1364852736 | bytes 7667720 | tf_op jit(solution)/shard_map/dot_general | solution.py:58
  157.0 6.8 %convolution_add_fusion.1 = f32[768,1152]{1,0:T(8,128)} fusion(f32[768,1152]{1,0:T(8,128)} %fusion.37, bf16[768,1152]{1,0:T(8,128)(2,1)} %copy-done.3, f32[768,768]{1,0:T(8,128)} %copy-done.4, f32[]{:T(128)} %bitcast.80, f32[]{:T(128)} %bitcast), kind=kOutput, calls=%fused_computation.20 | convolution fusion | flops 1363378176 | bytes 11206664 | tf_op jit(solution)/shard_map/dot_general | solution.py:58
  163.9 138.4 %all-reduce = (f32[]{:T(128)}, f32[]{:T(128)}, f32[]{:T(128)}) all-reduce(f32[]{:T(128)S(6)} %add.106, f32[]{:T(128)S(6)} %add.115, f32[]{:T(128)S(6)} %add.117), channel_id=1, replica_groups=mesh['blk'=128,'rep'=2] {'blk','rep'}, use_global_device_ids=true, to_apply=%region_3.4 | all-reduce | flops 3 | bytes 24 | tf_op jit(solution)/shard_map/psum | solution.py:65
  304.2 5.2 %fusion.12 = (f32[768]{0:T(1024)S(1)}, f32[768,1152]{1,0:T(8,128)S(1)}) fusion(bf16[1,768,1152]{2,1,0:T(8,128)(2,1)S(1)} %copy-done.1, f32[768]{0:T(1024)S(1)} %add_rsqrt_fusion.1, f32[]{:T(128)} %bitcast, f32[768,1152]{1,0:T(8,128)} %convolution_add_fusion.1, bf16[768,1152]{1,0:T(8,128)(2,1)} %copy-done.2, f32[]{:T(128)} %bitcast.79, f32[768,768]{1,0:T(8,128)} %copy-done.5), kind=kOutput, calls=%fused_computation.21 | convolution fusion | flops 1367801088 | bytes 12982280 | tf_op jit(solution)/shard_map/dot_general | solution.py:58
  309.4 2.5 fusion.15
  311.8 2.6 fusion.18
  314.4 4.5 %fusion.21 = f32[1,768,1152]{2,1,0:T(8,128)} fusion(f32[768,1152]{1,0:T(8,128)} %collective-permute-done.4, bf16[1,768,1152]{2,1,0:T(8,128)(2,1)S(1)} %copy-done, f32[768]{0:T(1024)S(1)} %fusion.18, f32[768]{0:T(1024)S(1)} %add_rsqrt_fusion), kind=kLoop, calls=%fused_computation.30 | loop fusion | flops 4423680 | bytes 8853504 | tf_op jit(solution)/shard_map/broadcast_in_dim | solution.py:72
  (17 shorter events, 0.0 us)
Async XLA Ops:
  0.6 5.6 %copy-start = (bf16[1,768,1152]{2,1,0:T(8,128)(2,1)S(1)}, bf16[1,768,1152]{2,1,0:T(8,128)(2,1)}, u32[]{:S(2)}) copy-start(bf16[1,768,1152]{2,1,0:T(8,128)(2,1)} %param.5) | copy-start | bytes 5308420
  0.6 5.6 %copy-start.1 = (bf16[1,768,1152]{2,1,0:T(8,128)(2,1)S(1)}, bf16[1,768,1152]{2,1,0:T(8,128)(2,1)}, u32[]{:S(2)}) copy-start(bf16[1,768,1152]{2,1,0:T(8,128)(2,1)} %param.4) | copy-start | bytes 5308420
  12.7 64.2 %collective-permute-start.2 = (f32[768,1152]{1,0:T(8,128)S(1)}, f32[768,1152]{1,0:T(8,128)S(1)}, u32[]{:S(2)}, u32[]{:S(2)}) collective-permute-start(f32[768,1152]{1,0:T(8,128)S(1)} %convolution_multiply_fusion.2), channel_id=1, source_target_pairs={{254,0},{0,2},{2,4},{4,6},{6,8},{8,10},{10,12},{12,14},{14,16},{16... | collective-permute-start | bytes 10616840 | tf_op jit(solution)/shard_map/ppermute | solution.py:12
  13.1 59.5 %collective-permute-start = (bf16[768,1152]{1,0:T(8,128)(2,1)S(1)}, bf16[768,1152]{1,0:T(8,128)(2,1)S(1)}, u32[]{:S(2)}, u32[]{:S(2)}) collective-permute-start(bf16[768,1152]{1,0:T(8,128)(2,1)S(1)} %fusion.4), channel_id=1, source_target_pairs={{254,0},{0,2},{2,4},{4,6},{6,8},{8,10},{10,12},{12,14},{14,16},{16... | collective-permute-start | bytes 5308424 | tf_op jit(solution)/shard_map/ppermute | solution.py:12
  72.6 6.4 %copy-start.3 = (bf16[768,1152]{1,0:T(8,128)(2,1)}, bf16[768,1152]{1,0:T(8,128)(2,1)S(1)}, u32[]{:S(2)}) copy-start(bf16[768,1152]{1,0:T(8,128)(2,1)S(1)} %collective-permute-done) | copy-start | bytes 5308420
  76.8 2.0 copy-start.4
  78.9 66.2 %collective-permute-start.3 = (f32[768,1152]{1,0:T(8,128)S(1)}, f32[768,1152]{1,0:T(8,128)S(1)}, u32[]{:S(2)}, u32[]{:S(2)}) collective-permute-start(f32[768,1152]{1,0:T(8,128)S(1)} %fusion.10), channel_id=1, source_target_pairs={{254,0},{0,2},{2,4},{4,6},{6,8},{8,10},{10,12},{12,14},{14,16},{16... | collective-permute-start | bytes 10616840 | tf_op jit(solution)/shard_map/ppermute | solution.py:12
  79.0 59.8 %collective-permute-start.1 = (bf16[768,1152]{1,0:T(8,128)(2,1)S(1)}, bf16[768,1152]{1,0:T(8,128)(2,1)S(1)}, u32[]{:S(2)}, u32[]{:S(2)}) collective-permute-start(bf16[768,1152]{1,0:T(8,128)(2,1)S(1)} %collective-permute-done), channel_id=1, source_target_pairs={{254,0},{0,2},{2,4},{4,6},{6,8},{8,10},{10,12},{12,14},{14,16},{16... | collective-permute-start | bytes 5308424 | tf_op jit(solution)/shard_map/ppermute | solution.py:12
  138.8 4.3 %copy-start.2 = (bf16[768,1152]{1,0:T(8,128)(2,1)}, bf16[768,1152]{1,0:T(8,128)(2,1)S(1)}, u32[]{:S(2)}) copy-start(bf16[768,1152]{1,0:T(8,128)(2,1)S(1)} %collective-permute-done.1) | copy-start | bytes 5308420
  143.1 1.9 copy-start.5
  147.2 164.7 %collective-permute-start.4 = (f32[768,1152]{1,0:T(8,128)}, f32[768,1152]{1,0:T(8,128)}, u32[]{:S(2)}, u32[]{:S(2)}) collective-permute-start(f32[768,1152]{1,0:T(8,128)} %add.113), channel_id=1, source_target_pairs={{4,0},{6,2},{8,4},{10,6},{12,8},{14,10},{16,12},{18,14},{20,16},{2... | collective-permute-start | bytes 10616840 | tf_op jit(solution)/shard_map/ppermute | solution.py:12
where the time goes:
time: 327 us; the launch traced here: 322 us
  blocking collectives  138 us (42%)
  waiting for transfers between devices  116 us (35%)
  matrix products  34.7 us (11%)
  other arithmetic  15.8 us (5%)
  between operations  13.4 us (4%)
  starting transfers between devices  3.63 us (1%)
    psum x1, blocking collectives, body(): lax.psum((total, dtemp, dbias), ('blk', 'rep'))  138 us
    ppermute x5, waiting for transfers between devices, shifted(): return lax.ppermute(block, axis, route)  116 us
    dot_general x3, matrix products, body(): jnp.dot(slope_low, moving, preferred_element_type=jnp.float32)  15.9 us
    dot_general x3, matrix products, pair_block(): lax.dot_general(left, right, (((1,), (1,)), ((), ())), preferred_element_...  12.9 us
  transfers between devices with their start and end apart: 5, of which 2 were waited for; matrix products, arithmetic and copies ran while one was open for 9% of the time, Pallas kernels for 0%

commit v1 on v0

v1 whole, which is shorter than its diff:
```python
import functools

import jax
import jax.numpy as jnp
from jax import lax
from jax.experimental import pallas as pl
from jax.experimental.pallas import tpu as pltpu
from jax.sharding import PartitionSpec as P

SPANS = 3
TILE = 256
LOW = jnp.bfloat16
F32 = jnp.float32
VMEM_LIMIT = 16 * 1024 * 1024


def params():
    return pltpu.CompilerParams(vmem_limit_bytes=VMEM_LIMIT)


def cost(flops, moved, trans=0):
    return pl.CostEstimate(flops=0, bytes_accessed=0, transcendentals=0)


def smem():
    return pl.BlockSpec(memory_space=pltpu.SMEM)


def vmem():
    return pl.BlockSpec(memory_space=pltpu.VMEM)


def hbm():
    return pl.BlockSpec(memory_space=pltpu.HBM)


def near(*values):
    return [pltpu.with_memory_space_constraint(v, pltpu.VMEM) for v in values]


def far(*values):
    return [pltpu.with_memory_space_constraint(v, pltpu.HBM) for v in values]


def unit_rows(raw):
    scale = lax.rsqrt(jnp.sum(raw * raw, axis=-1, keepdims=True) + 1e-06)
    return raw * scale, scale


def dot_t(x, y):
    return lax.dot_general(x, y, (((1,), (1,)), ((), ())), preferred_element_type=F32)


def dot(x, y):
    return jnp.dot(x, y, preferred_element_type=F32)


def pieces(rows):
    return [slice(r, r + TILE) for r in range(0, rows, TILE)]


def fold(values):
    rows, width = values.shape
    part = jnp.sum(values.reshape(rows // 8, 8, width), axis=0)
    return functools.reduce(jnp.add, [part[:, c : c + 128] for c in range(0, width, 128)])


def joined(p, q):
    return p + q + p * q


def log_fold(grown):
    rows, width = grown.shape
    groups = grown.reshape(rows // 64, 8, 8, width)
    parts = [groups[:, i] for i in range(8)]
    while len(parts) > 1:
        parts = [joined(p, q) for p, q in zip(parts[::2], parts[1::2])]
    return fold(jnp.log1p(parts[0]).reshape(rows // 8, width))


def share(grown):
    whole = 1.0 + grown
    inverse = pl.reciprocal(whole, approx=True)
    inverse = inverse * (2.0 - whole * inverse)
    return grown * inverse


def sums_of(grown, slope, raw):
    return log_fold(grown), fold(slope * raw), fold(slope)


def put_sums(sums_in, sums_ref, total, weight):
    for k in range(3):
        rows = slice(8 * k, 8 * k + 8)
        sums_ref[rows, :] = (sums_in[rows, :] if sums_in is not None else 0.0) + weight * total[k]


def unit_kernel(even_ref, image_ref, text_ref, a_ref, b_ref, slots, sems):
    even = even_ref[0] == 1
    parts = pieces(a_ref.shape[0])

    @pl.when(even)
    def _():
        for k, ref in enumerate((image_ref, text_ref)):
            for c, rows in enumerate(parts):
                pltpu.make_async_copy(ref.at[0, rows], slots.at[k, c], sems.at[k, c]).start()

    @pl.when(jnp.logical_not(even))
    def _():
        for k, ref in enumerate((text_ref, image_ref)):
            for c, rows in enumerate(parts):
                pltpu.make_async_copy(ref.at[0, rows], slots.at[k, c], sems.at[k, c]).start()

    for k, out_ref in enumerate((a_ref, b_ref)):
        for c, rows in enumerate(parts):
            pltpu.make_async_copy(image_ref.at[0, rows], slots.at[k, c], sems.at[k, c]).wait()
            out_ref[rows, :] = unit_rows(slots[k, c].astype(F32))[0].astype(LOW)


def unit_blocks(even, image, text):
    _, rows, width = image.shape
    full = pltpu.VMEM((rows, width), LOW)
    count = rows // TILE
    return pl.pallas_call(
        unit_kernel,
        in_specs=[smem(), hbm(), hbm()],
        out_specs=[vmem()] * 2,
        out_shape=[full] * 2,
        scratch_shapes=[
            pltpu.VMEM((2, count, TILE, width), LOW),
            pltpu.SemaphoreType.DMA((2, count)),
        ],
        compiler_params=params(),
        cost_estimate=cost(rows * width * 8, rows * width * 12),
        name="unit_blocks",
    )(even, *far(image, text))


def own_kernel(scalar_ref, a_ref, b_ref, slope_ref, sums_ref):
    temper, bias = scalar_ref[0], scalar_ref[1]
    total = None
    for rows in pieces(a_ref.shape[0]):
        raw = dot_t(a_ref[rows, :], b_ref[...])
        logits = temper * raw + bias
        row = lax.broadcasted_iota(jnp.int32, raw.shape, 0) + rows.start
        diagonal = row == lax.broadcasted_iota(jnp.int32, raw.shape, 1)
        grown = jnp.exp(jnp.where(diagonal, -logits, logits))
        part = share(grown)
        slope = jnp.where(diagonal, -part, part)
        slope_ref[rows, :] = slope.astype(LOW)
        part = sums_of(grown, slope, raw)
        total = part if total is None else [p + q for p, q in zip(total, part)]
    put_sums(None, sums_ref, total, 1.0)


def own_slopes(scalars, a, b):
    rows, width = a.shape
    return pl.pallas_call(
        own_kernel,
        in_specs=[smem(), vmem(), vmem()],
        out_specs=[vmem(), vmem()],
        out_shape=[pltpu.VMEM((rows, rows), LOW), pltpu.VMEM((24, 128), F32)],
        compiler_params=params(),
        cost_estimate=cost(2 * rows * rows * width, rows * width * 6, 3 * rows * rows),
        name="own_slopes",
    )(scalars, *near(a, b))


def pair_slopes(temper, bias, x, y):
    raw = dot_t(x, y)
    grown = jnp.exp(temper * raw + bias)
    return raw, grown, share(grown)


def slopes_kernel(scalar_ref, x_ref, y_ref, sums_in, slope_ref, sums_ref, *, weight):
    total = None
    for rows in pieces(x_ref.shape[0]):
        raw, grown, slope = pair_slopes(scalar_ref[0], scalar_ref[1], x_ref[rows, :], y_ref[...])
        slope_ref[rows, :] = slope.astype(LOW)
        part = sums_of(grown, slope, raw)
        total = part if total is None else [p + q for p, q in zip(total, part)]
    put_sums(sums_in, sums_ref, total, weight)


def slopes(scalars, x, y, sums, weight):
    rows, width = x.shape
    other = y.shape[0]
    return pl.pallas_call(
        functools.partial(slopes_kernel, weight=weight),
        in_specs=[smem(), vmem(), vmem(), vmem()],
        out_specs=[vmem(), vmem()],
        out_shape=[pltpu.VMEM((rows, other), LOW), pltpu.VMEM((24, 128), F32)],
        compiler_params=params(),
        cost_estimate=cost(2 * rows * other * width, (rows + other) * width * 4, 3 * rows * other),
        name="slopes",
    )(scalars, *near(x, y, sums))


def late_kernel(even_ref, scalar_ref, x_ref, y_ref, w_ref, sums_in, slope_ref, sums_ref):
    temper, bias = scalar_ref[0], scalar_ref[1]
    total = None
    for rows in pieces(x_ref.shape[0]):
        raw, grown, slope = pair_slopes(temper, bias, x_ref[rows, :], y_ref[...])
        slope_ref[rows, :] = slope.astype(LOW)
        part = sums_of(grown, slope, raw)
        total = part if total is None else [p + q for p, q in zip(total, part)]
    put_sums(sums_in, sums_ref, total, 1.0)
    half = x_ref.shape[0] // 2

    def rest(left, right):
        raw, grown, slope = pair_slopes(temper, bias, left, right)
        put_sums(sums_ref, sums_ref, sums_of(grown, slope, raw), 1.0)

    @pl.when(even_ref[0] == 1)
    def _():
        rest(w_ref[...], y_ref[half:, :])

    @pl.when(even_ref[0] == 0)
    def _():
        rest(y_ref[...], w_ref[:half, :])


def late_slopes(even, scalars, x, y, w, sums):
    rows, width = x.shape
    return pl.pallas_call(
        late_kernel,
        in_specs=[smem(), smem()] + [vmem()] * 4,
        out_specs=[vmem(), vmem()],
        out_shape=[pltpu.VMEM((rows, rows), LOW), pltpu.VMEM((24, 128), F32)],
        compiler_params=params(),
        cost_estimate=cost(3 * rows * rows * width, rows * width * 8, 4 * rows * rows),
        name="late_slopes",
    )(even, scalars, *near(x, y, w, sums))


def start_kernel(own_ref, a_ref, b_ref, other_ref, e_ref, ga_ref, gb_ref):
    for rows in pieces(a_ref.shape[0]):
        ga_ref[rows, :] = dot(own_ref[rows, :], b_ref[...])
        term = lax.dot_general(
            own_ref[:, rows], a_ref[...], (((0,), (0,)), ((), ())), preferred_element_type=F32
        )
        gb_ref[rows, :] = term + dot(other_ref[rows, :], e_ref[...])


def start_grads(own, a, b, other, e):
    rows, width = a.shape
    grad = pltpu.VMEM((rows, width), F32)
    return pl.pallas_call(
        start_kernel,
        in_specs=[vmem()] * 5,
        out_specs=[vmem()] * 2,
        out_shape=[grad, grad],
        compiler_params=params(),
        cost_estimate=cost(6 * rows * rows * width, rows * width * 16),
        name="start_grads",
    )(*near(own, a, b, other, e))


def back(grad, raw):
    unit, scale = unit_rows(raw.astype(F32))
    return (grad - unit * jnp.sum(unit * grad, axis=-1, keepdims=True)) * scale


def start_raw(first, even_in, odd_in, slots, sems, parts):
    @pl.when(first)
    def _():
        for c, rows in enumerate(parts):
            pltpu.make_async_copy(even_in.at[0, rows], slots.at[c], sems.at[0, c]).start()

    @pl.when(jnp.logical_not(first))
    def _():
        for c, rows in enumerate(parts):
            pltpu.make_async_copy(odd_in.at[0, rows], slots.at[c], sems.at[0, c]).start()


def start_out(first, c, rows, even_out, odd_out, slots, sems):
    @pl.when(first)
    def _():
        pltpu.make_async_copy(slots.at[c], even_out.at[0, rows], sems.at[1, c]).start()

    @pl.when(jnp.logical_not(first))
    def _():
        pltpu.make_async_copy(slots.at[c], odd_out.at[0, rows], sems.at[1, c]).start()


def b_kernel(
    even_ref, scalar_ref, image_ref, text_ref, s_ref, p_ref, g_ref,
    image_out, text_out, raws, slots, sems,
):
    even = even_ref[0] == 1
    parts = pieces(g_ref.shape[0])
    start_raw(even, text_ref, image_ref, raws, sems, parts)
    for c, rows in enumerate(parts):
        total = g_ref[rows, :] + dot(s_ref[rows, :], p_ref[...])
        pltpu.make_async_copy(text_ref.at[0, rows], raws.at[c], sems.at[0, c]).wait()
        slots[c] = back(scalar_ref[0] * total, raws[c])
        start_out(even, c, rows, text_out, image_out, slots, sems)
    for c, rows in enumerate(parts):
        pltpu.make_async_copy(slots.at[c], text_out.at[0, rows], sems.at[1, c]).wait()


def finish_b(even, scalars, image, text, s, p, grad):
    rows, width = grad.shape
    out = pltpu.HBM((1, rows, width), F32)
    count = rows // TILE
    return pl.pallas_call(
        b_kernel,
        in_specs=[smem(), smem(), hbm(), hbm()] + [vmem()] * 3,
        out_specs=[hbm()] * 2,
        out_shape=[out, out],
        scratch_shapes=[
            pltpu.VMEM((count, TILE, width), LOW),
            pltpu.VMEM((count, TILE, width), F32),
            pltpu.SemaphoreType.DMA((2, count)),
        ],
        compiler_params=params(),
        cost_estimate=cost(2 * rows * rows * width, rows * width * 14),
        name="finish_b",
    )(even, scalars, *far(image, text), *near(s, p, grad))


def a_kernel(
    even_ref, scalar_ref, image_ref, text_ref, a_ref, f_ref, q_ref, g_ref, _image, _text,
    image_out, text_out, raws, slots, sems,
):
    even = even_ref[0] == 1
    temper, bias = scalar_ref[0], scalar_ref[1]
    parts = pieces(g_ref.shape[0])
    start_raw(even, image_ref, text_ref, raws, sems, parts)
    for c, rows in enumerate(parts):
        total = g_ref[rows, :]
        for y_ref in (f_ref, q_ref):
            slope = pair_slopes(temper, bias, a_ref[rows, :], y_ref[...])[2]
            total = total + dot(slope.astype(LOW), y_ref[...])
        pltpu.make_async_copy(image_ref.at[0, rows], raws.at[c], sems.at[0, c]).wait()
        slots[c] = back(temper * total, raws[c])
        start_out(even, c, rows, image_out, text_out, slots, sems)
    for c, rows in enumerate(parts):
        pltpu.make_async_copy(slots.at[c], image_out.at[0, rows], sems.at[1, c]).wait()


def finish_a(even, scalars, image, text, a, f, q, grad, image_out, text_out):
    rows, width = grad.shape
    out = pltpu.HBM((1, rows, width), F32)
    count = rows // TILE
    return pl.pallas_call(
        a_kernel,
        in_specs=[smem(), smem(), hbm(), hbm()] + [vmem()] * 4 + [hbm()] * 2,
        out_specs=[hbm()] * 2,
        out_shape=[out, out],
        input_output_aliases={8: 0, 9: 1},
        scratch_shapes=[
            pltpu.VMEM((count, TILE, width), LOW),
            pltpu.VMEM((count, TILE, width), F32),
            pltpu.SemaphoreType.DMA((2, count)),
        ],
        compiler_params=params(),
        cost_estimate=cost(8 * rows * rows * width, rows * width * 20),
        name="finish_a",
    )(even, scalars, *far(image, text), *near(a, f, q, grad), *far(image_out, text_out))


def partner(block):
    count = lax.axis_size("blk")
    return lax.ppermute(block, "blk", [(i, i ^ 1) for i in range(count)])


def outward(block):
    count = lax.axis_size("blk")
    return lax.ppermute(block, "blk", [(i, (i + (2 if i % 2 else -2)) % count) for i in range(count)])


def inward(block):
    count = lax.axis_size("blk")
    return lax.ppermute(block, "blk", [(i, (i + (1 if i % 2 else -1)) % count) for i in range(count)])


def swap(sums, mask):
    total = lax.axis_size("blk") * lax.axis_size("rep")
    route = [(i, i ^ mask) for i in range(total)]
    return sums + lax.ppermute(sums, ("blk", "rep"), route)


def after(value, *others):
    return lax.optimization_barrier((value, *others))[0]


def body(image, text, log_temp, bias):
    _, rows, width = image.shape
    temper = jnp.exp(log_temp)
    scalars = jnp.concatenate([temper, bias])
    even = (lax.rem(lax.axis_index("blk"), 2) == 0).astype(jnp.int32).reshape(1)

    a, b = unit_blocks(even, image, text)
    p = outward(a)
    e = partner(b)
    w = partner(a)

    s_own, sums = own_slopes(scalars, a, b)
    q = inward(e)
    s_e, sums = slopes(scalars, b, e, sums, 0.5)
    grad_a, grad_b = start_grads(after(s_own, sums), a, b, s_e, e)
    s_p, sums = late_slopes(even, scalars, b, after(p, grad_b), w, sums)
    f = partner(after(p, sums))
    small = jnp.sum(sums.reshape(3, 8, 128), axis=1)
    for mask in (2, 128, 64):
        small = swap(small, mask)
    small = after(small, q)
    total = swap(small, 16)
    image_out, text_out = finish_b(
        after(even, small), scalars, image, text, s_p, p, grad_b
    )
    small = after(total, image_out)
    for mask in (32,):
        small = swap(small, mask)
    total = swap(small, 8)
    grad_image, grad_text = finish_a(
        after(even, small), scalars, image, text, a, f, q, grad_a, image_out, text_out
    )
    small = after(total, grad_image)
    for mask in (4, 1):
        small = swap(small, mask)

    pairs = float(lax.axis_size("rep") * lax.axis_size("blk") * rows * SPANS * rows)
    small = jnp.sum(small, axis=1) / pairs
    return (small[0:1], grad_image, grad_text, small[1:2] * temper, small[2:3])


def solution(mesh):
    return jax.shard_map(
        body,
        mesh=mesh,
        in_specs=(P("rep", "blk", None), P("rep", "blk", None), P(), P()),
        out_specs=(P(), P("rep", "blk", None), P("rep", "blk", None), P(), P()),
        check_vma=False,
    )
```

time: 327 us -> 89.3 us (0.27); the launches traced: 322 us -> 89.2 us
  blocking collectives: 138 us -> 0 us
  waiting for transfers between devices: 116 us -> 23.5 us
  matrix products: 34.7 us -> 0 us
  Pallas kernels: 0 us -> 33.3 us
  starting transfers between devices: 3.63 us -> 27.7 us
  other arithmetic: 15.8 us -> 0.24 us
  between operations: 13.4 us -> 3.87 us
    psum x1 -> x0, blocking collectives: 138 us -> none  [body(): lax.psum((total, dtemp, dbias), ('blk', 'rep'))]
    ppermute x5 -> x13, waiting for transfers between devices: 116 us -> 23.5 us  [the longest x8 14.8 us: swap(): return sums + lax.ppermute(sums, ('blk', 'rep'), route)]
    dot_general x9 -> x0, matrix products: 34.7 us -> none  [the longest x3 15.9 us: body(): jnp.dot(slope_low, moving, preferred_element_type=jnp.float32)]
    pallas_call x0 -> x7, Pallas kernels: none -> 33.3 us  [the longest x1 10.4 us: finish_a(): pl.pallas_call(a_kernel, in_specs=[smem(), smem(), hbm(), hbm()] + [vmem(...]
    ppermute x5 -> x13, starting transfers between devices: 3.63 us -> 27.7 us  [the longest x8 25.8 us: swap(): return sums + lax.ppermute(sums, ('blk', 'rep'), route)]
    broadcast_in_dim x2 -> x0, other arithmetic: 6.93 us -> none  [the longest x1 4.46 us: body(): grad_text = unit_back(text_grad, unit_text, text_scale)[None]]
    reduce_sum x3 -> x2, other arithmetic: 6.39 us -> 0.13 us  [the longest x1 0.11 us: body(): small = jnp.sum(small, axis=1) / pairs]
  transfers between devices with their start and end apart: 5 -> 13, of which waited for: 2 -> 8; matrix products, arithmetic and copies ran while one was open for 9% -> 0% of each run, Pallas kernels for 0% -> 35%
where the time goes in v1:
time: 89.3 us; the launch traced here: 89.2 us
  Pallas kernels  33.3 us (37%)
  starting transfers between devices  27.7 us (31%)
  waiting for transfers between devices  23.5 us (26%)
  between operations  3.87 us (4%)
    ppermute x8, starting transfers between devices, swap(): return sums + lax.ppermute(sums, ('blk', 'rep'), route)  25.8 us
    ppermute x8, waiting for transfers between devices, swap(): return sums + lax.ppermute(sums, ('blk', 'rep'), route)  14.8 us
    pallas_call x1, Pallas kernels, finish_a(): pl.pallas_call(a_kernel, in_specs=[smem(), smem(), hbm(), hbm()] + [vmem(...  10.4 us
    ppermute x1, waiting for transfers between devices, outward(): lax.ppermute(block, 'blk', [(i, (i + (2 if i % 2 else -2)) % count) for i...  7.9 us
    pallas_call x1, Pallas kernels, finish_b(): pl.pallas_call(b_kernel, in_specs=[smem(), smem(), hbm(), hbm()] + [vmem(...  5.02 us
    pallas_call x1, Pallas kernels, start_grads(): pl.pallas_call(start_kernel, in_specs=[vmem()] * 5, out_specs=[vmem()] *...  4.83 us
    pallas_call x1, Pallas kernels, late_slopes(): pl.pallas_call(late_kernel, in_specs=[smem(), smem()] + [vmem()] * 4, out...  4.78 us
    pallas_call x1, Pallas kernels, own_slopes(): pl.pallas_call(own_kernel, in_specs=[smem(), vmem(), vmem()], out_specs=[...  3 us
  transfers between devices with their start and end apart: 13, of which 8 were waited for; matrix products, arithmetic and copies ran while one was open for 0% of the time, Pallas kernels for 35%

profile of v1, /device:TPU:52, one launch (start us, length us, event | category | flops | bytes accessed | tf_op | source)
XLA Modules:
  0.0 89.2 jit_solution(7981429031528430371)
XLA Ops:
  0.6 2.3 %unit_blocks.1 = (bf16[768,1152]{1,0:T(8,128)(2,1)S(1)}, bf16[768,1152]{1,0:T(8,128)(2,1)S(1)}) custom-call(s32[1]{0:T(128)} %bitcast.even_ref, bf16[1,768,1152]{2,1,0:T(8,128)(2,1)} %image_ref.5, bf16[1,768,1152]{2,1,0:T(8,128)(2,1)} %text_ref.5), custom_call_target="tpu_custom_call" | custom-call | tf_op jit(solution)/shard_map/unit_blocks/pallas_call | solution.py:124
  3.1 0.5 collective-permute-start
  3.6 1.0 %collective-permute-start.2 = (bf16[768,1152]{1,0:T(8,128)(2,1)S(1)}, bf16[768,1152]{1,0:T(8,128)(2,1)S(1)}, u32[]{:S(2)}, u32[]{:S(2)}) collective-permute-start(bf16[768,1152]{1,0:T(8,128)(2,1)S(1)} %get-tuple-element.28.a_ref), channel_id=1, source_target_pairs={{0,2},{2,0},{4,6},{6,4},{8,10},{10,8},{12,14},{14,12},{16,18},{18,... | collective-permute-start | bytes 5308424 | tf_op jit(solution)/shard_map/ppermute | solution.py:365
  5.9 0.8 collective-permute-done.1.y_ref.e_ref
  7.0 3.0 %own_slopes.1 = (bf16[768,768]{1,0:T(8,128)(2,1)S(1)}, f32[24,128]{1,0:T(8,128)S(1)}) custom-call(f32[2]{0:T(128)S(1)} %pad_maximum_fusion.scalar_ref, bf16[768,1152]{1,0:T(8,128)(2,1)S(1)} %get-tuple-element.28.a_ref, bf16[768,1152]{1,0:T(8,128)(2,1)S(1)} %get-tuple-element.27.b_ref.x_ref), custom_call_target="tpu_custom_call" | custom-call | tf_op jit(solution)/shard_map/own_slopes/pallas_call | solution.py:158
  10.0 2.9 %slopes.1 = (bf16[768,768]{1,0:T(8,128)(2,1)S(1)}, f32[24,128]{1,0:T(8,128)S(1)}) custom-call(f32[2]{0:T(128)S(1)} %pad_maximum_fusion.scalar_ref, bf16[768,1152]{1,0:T(8,128)(2,1)S(1)} %get-tuple-element.27.b_ref.x_ref, bf16[768,1152]{1,0:T(8,128)(2,1)S(1)} %collective-permute-done.1.y_ref.e_ref, f32[24,128]{1,0:T(8,128)S(1)} %get-tuple-element.30.sums_in), custom_call_target="tpu_custom_call" | custom-call | tf_op jit(solution)/shard_map/slopes/pallas_call | solution.py:188
  12.9 4.8 %start_grads.1 = (f32[768,1152]{1,0:T(8,128)S(1)}, f32[768,1152]{1,0:T(8,128)S(1)}) custom-call(bf16[768,768]{1,0:T(8,128)(2,1)S(1)} %get-tuple-element.32.own_ref, bf16[768,1152]{1,0:T(8,128)(2,1)S(1)} %get-tuple-element.28.a_ref, bf16[768,1152]{1,0:T(8,128)(2,1)S(1)} %get-tuple-element.27.b_ref.x_ref, bf16[768,768]{1,0:T(8,128)(2,1)S(1)} %get-tuple-element.33.other_ref, ...), custom_call_target="tpu_custom_call" | custom-call | tf_op jit(solution)/shard_map/start_grads/pallas_call | solution.py:248
  17.8 7.9 %collective-permute-done.y_ref.p_ref = bf16[768,1152]{1,0:T(8,128)(2,1)S(1)} collective-permute-done((bf16[768,1152]{1,0:T(8,128)(2,1)S(1)}, bf16[768,1152]{1,0:T(8,128)(2,1)S(1)}, u32[]{:S(2)}, u32[]{:S(2)}) %collective-permute-start) | collective-permute-done | bytes 1769504 | tf_op jit(solution)/shard_map/ppermute | solution.py:370
  25.7 4.8 %late_slopes.1 = (bf16[768,768]{1,0:T(8,128)(2,1)S(1)}, f32[24,128]{1,0:T(8,128)S(1)}) custom-call(s32[1]{0:T(128)} %bitcast.even_ref, f32[2]{0:T(128)S(1)} %pad_maximum_fusion.scalar_ref, bf16[768,1152]{1,0:T(8,128)(2,1)S(1)} %get-tuple-element.27.b_ref.x_ref, bf16[768,1152]{1,0:T(8,128)(2,1)S(1)} %collective-permute-done.y_ref.p_ref, ...), custom_call_target="tpu_custom_call" | custom-call | tf_op jit(solution)/shard_map/late_slopes/pallas_call | solution.py:225
  30.6 0.6 collective-permute-start.3
  31.2 3.1 %collective-permute-done.3 = f32[3,128]{1,0:T(4,128)S(1)} collective-permute-done((f32[3,128]{1,0:T(4,128)S(1)}, f32[3,128]{1,0:T(4,128)S(1)}, u32[]{:S(2)}, u32[]{:S(2)}) %collective-permute-start.3) | collective-permute-done | bytes 1568 | tf_op jit(solution)/shard_map/ppermute | solution.py:381
  34.3 6.3 %collective-permute-start.4 = (f32[3,128]{1,0:T(4,128)S(1)}, f32[3,128]{1,0:T(4,128)S(1)}, u32[]{:S(2)}, u32[]{:S(2)}) collective-permute-start(f32[3,128]{1,0:T(4,128)S(1)} %add.24), channel_id=1, source_target_pairs={{0,128},{1,129},{2,130},{3,131},{4,132},{5,133},{6,134},{7,135},{8... | collective-permute-start | bytes 4616 | tf_op jit(solution)/shard_map/ppermute | solution.py:381
  40.5 1.6 %collective-permute-done.4 = f32[3,128]{1,0:T(4,128)S(1)} collective-permute-done((f32[3,128]{1,0:T(4,128)S(1)}, f32[3,128]{1,0:T(4,128)S(1)}, u32[]{:S(2)}, u32[]{:S(2)}) %collective-permute-start.4) | collective-permute-done | bytes 1568 | tf_op jit(solution)/shard_map/ppermute | solution.py:381
  42.1 2.9 %collective-permute-start.5 = (f32[3,128]{1,0:T(4,128)S(1)}, f32[3,128]{1,0:T(4,128)S(1)}, u32[]{:S(2)}, u32[]{:S(2)}) collective-permute-start(f32[3,128]{1,0:T(4,128)S(1)} %add.25), channel_id=1, source_target_pairs={{0,64},{1,65},{2,66},{3,67},{4,68},{5,69},{6,70},{7,71},{8,72},{9,... | collective-permute-start | bytes 4616 | tf_op jit(solution)/shard_map/ppermute | solution.py:381
  45.0 1.6 %collective-permute-done.5 = f32[3,128]{1,0:T(4,128)S(1)} collective-permute-done((f32[3,128]{1,0:T(4,128)S(1)}, f32[3,128]{1,0:T(4,128)S(1)}, u32[]{:S(2)}, u32[]{:S(2)}) %collective-permute-start.5) | collective-permute-done | bytes 1568 | tf_op jit(solution)/shard_map/ppermute | solution.py:381
  47.1 5.0 %finish_b.1 = (f32[1,768,1152]{2,1,0:T(8,128)}, f32[1,768,1152]{2,1,0:T(8,128)}) custom-call(s32[1]{0:T(128)} %bitcast.even_ref, f32[2]{0:T(128)S(1)} %pad_maximum_fusion.scalar_ref, bf16[1,768,1152]{2,1,0:T(8,128)(2,1)} %image_ref.5, bf16[1,768,1152]{2,1,0:T(8,128)(2,1)} %text_ref.5, bf16[768,768]{1,0:T(8,128)(2,1)S(1)} %get-tuple-element.39.s_ref, ...), custom_call_target="tpu_custom_call" | custom-call | tf_op jit(solution)/shard_map/finish_b/pallas_call | solution.py:306
  52.2 1.1 %collective-permute-start.8 = (f32[3,128]{1,0:T(4,128)S(1)}, f32[3,128]{1,0:T(4,128)S(1)}, u32[]{:S(2)}, u32[]{:S(2)}) collective-permute-start(f32[3,128]{1,0:T(4,128)S(1)} %add.27), channel_id=1, source_target_pairs={{0,32},{1,33},{2,34},{3,35},{4,36},{5,37},{6,38},{7,39},{8,40},{9,... | collective-permute-start | bytes 4616 | tf_op jit(solution)/shard_map/ppermute | solution.py:381
  53.3 2.6 %collective-permute-done.8 = f32[3,128]{1,0:T(4,128)S(1)} collective-permute-done((f32[3,128]{1,0:T(4,128)S(1)}, f32[3,128]{1,0:T(4,128)S(1)}, u32[]{:S(2)}, u32[]{:S(2)}) %collective-permute-start.8) | collective-permute-done | bytes 1568 | tf_op jit(solution)/shard_map/ppermute | solution.py:381
  55.8 13.1 %collective-permute-start.9 = (f32[3,128]{1,0:T(4,128)S(1)}, f32[3,128]{1,0:T(4,128)S(1)}, u32[]{:S(2)}, u32[]{:S(2)}) collective-permute-start(f32[3,128]{1,0:T(4,128)S(1)} %add.28), channel_id=1, source_target_pairs={{0,8},{1,9},{2,10},{3,11},{4,12},{5,13},{6,14},{7,15},{8,0},{9,1},... | collective-permute-start | bytes 4616 | tf_op jit(solution)/shard_map/ppermute | solution.py:381
  69.0 10.4 %finish_a.1 = (f32[1,768,1152]{2,1,0:T(8,128)}, f32[1,768,1152]{2,1,0:T(8,128)}) custom-call(s32[1]{0:T(128)} %bitcast.even_ref, f32[2]{0:T(128)S(1)} %pad_maximum_fusion.scalar_ref, bf16[1,768,1152]{2,1,0:T(8,128)(2,1)} %image_ref.5, bf16[1,768,1152]{2,1,0:T(8,128)(2,1)} %text_ref.5, ...), custom_call_target="tpu_custom_call", output_to_operand_aliasing={{0}: (8, {}), {1}: (9, {})} | custom-call | tf_op jit(solution)/shard_map/finish_a/pallas_call | solution.py:346
  79.5 3.6 %collective-permute-done.11 = f32[3,128]{1,0:T(4,128)S(1)} collective-permute-done((f32[3,128]{1,0:T(4,128)S(1)}, f32[3,128]{1,0:T(4,128)S(1)}, u32[]{:S(2)}, u32[]{:S(2)}) %collective-permute-start.11) | collective-permute-done | bytes 1568 | tf_op jit(solution)/shard_map/ppermute | solution.py:381
  83.1 1.2 %collective-permute-start.12 = (f32[3,128]{1,0:T(4,128)S(1)}, f32[3,128]{1,0:T(4,128)S(1)}, u32[]{:S(2)}, u32[]{:S(2)}) collective-permute-start(f32[3,128]{1,0:T(4,128)S(1)} %add.30), channel_id=1, source_target_pairs={{0,1},{1,0},{2,3},{3,2},{4,5},{5,4},{6,7},{7,6},{8,9},{9,8},{10,11... | collective-permute-start | bytes 4616 | tf_op jit(solution)/shard_map/ppermute | solution.py:381
  84.3 2.4 %collective-permute-done.12 = f32[3,128]{1,0:T(4,128)S(1)} collective-permute-done((f32[3,128]{1,0:T(4,128)S(1)}, f32[3,128]{1,0:T(4,128)S(1)}, u32[]{:S(2)}, u32[]{:S(2)}) %collective-permute-start.12) | collective-permute-done | bytes 1568 | tf_op jit(solution)/shard_map/ppermute | solution.py:381
  86.8 0.6 fusion
  (21 shorter events, 1.2 us)
Async XLA Ops:
  3.0 3.8 %collective-permute-start.1 = (bf16[768,1152]{1,0:T(8,128)(2,1)S(1)}, bf16[768,1152]{1,0:T(8,128)(2,1)S(1)}, u32[]{:S(2)}, u32[]{:S(2)}) collective-permute-start(bf16[768,1152]{1,0:T(8,128)(2,1)S(1)} %get-tuple-element.27.b_ref.x_ref), channel_id=1, source_target_pairs={{0,2},{2,0},{4,6},{6,4},{8,10},{10,8},{12,14},{14,12},{16,18},{18,... | collective-permute-start | bytes 5308424 | tf_op jit(solution)/shard_map/ppermute | solution.py:365
  3.1 22.6 %collective-permute-start = (bf16[768,1152]{1,0:T(8,128)(2,1)S(1)}, bf16[768,1152]{1,0:T(8,128)(2,1)S(1)}, u32[]{:S(2)}, u32[]{:S(2)}) collective-permute-start(bf16[768,1152]{1,0:T(8,128)(2,1)S(1)} %get-tuple-element.28.a_ref), channel_id=1, source_target_pairs={{0,252},{2,6},{4,0},{6,10},{8,4},{10,14},{12,8},{14,18},{16,12},{1... | collective-permute-start | bytes 5308424 | tf_op jit(solution)/shard_map/ppermute | solution.py:370
  3.6 22.1 %collective-permute-start.2 = (bf16[768,1152]{1,0:T(8,128)(2,1)S(1)}, bf16[768,1152]{1,0:T(8,128)(2,1)S(1)}, u32[]{:S(2)}, u32[]{:S(2)}) collective-permute-start(bf16[768,1152]{1,0:T(8,128)(2,1)S(1)} %get-tuple-element.28.a_ref), channel_id=1, source_target_pairs={{0,2},{2,0},{4,6},{6,4},{8,10},{10,8},{12,14},{14,12},{16,18},{18,... | collective-permute-start | bytes 5308424 | tf_op jit(solution)/shard_map/ppermute | solution.py:365
  6.8 39.8 %collective-permute-start.6 = (bf16[768,1152]{1,0:T(8,128)(2,1)S(1)}, bf16[768,1152]{1,0:T(8,128)(2,1)S(1)}, u32[]{:S(2)}, u32[]{:S(2)}) collective-permute-start(bf16[768,1152]{1,0:T(8,128)(2,1)S(1)} %collective-permute-done.1.y_ref.e_ref), channel_id=1, source_target_pairs={{0,254},{2,4},{4,2},{6,8},{8,6},{10,12},{12,10},{14,16},{16,14},{1... | collective-permute-start | bytes 5308424 | tf_op jit(solution)/shard_map/ppermute | solution.py:375
  30.5 38.5 %collective-permute-start.10 = (bf16[768,1152]{1,0:T(8,128)(2,1)S(1)}, bf16[768,1152]{1,0:T(8,128)(2,1)S(1)}, u32[]{:S(2)}, u32[]{:S(2)}) collective-permute-start(bf16[768,1152]{1,0:T(8,128)(2,1)S(1)} %collective-permute-done.y_ref.p_ref), channel_id=1, source_target_pairs={{0,2},{2,0},{4,6},{6,4},{8,10},{10,8},{12,14},{14,12},{16,18},{18,... | collective-permute-start | bytes 5308424 | tf_op jit(solution)/shard_map/ppermute | solution.py:365
  30.6 3.7 %collective-permute-start.3 = (f32[3,128]{1,0:T(4,128)S(1)}, f32[3,128]{1,0:T(4,128)S(1)}, u32[]{:S(2)}, u32[]{:S(2)}) collective-permute-start(f32[3,128]{1,0:T(4,128)S(1)} %bitcast_reduce_fusion), channel_id=1, source_target_pairs={{0,2},{1,3},{2,0},{3,1},{4,6},{5,7},{6,4},{7,5},{8,10},{9,11},{10,... | collective-permute-start | bytes 4616 | tf_op jit(solution)/shard_map/ppermute | solution.py:381
  34.3 7.9 %collective-permute-start.4 = (f32[3,128]{1,0:T(4,128)S(1)}, f32[3,128]{1,0:T(4,128)S(1)}, u32[]{:S(2)}, u32[]{:S(2)}) collective-permute-start(f32[3,128]{1,0:T(4,128)S(1)} %add.24), channel_id=1, source_target_pairs={{0,128},{1,129},{2,130},{3,131},{4,132},{5,133},{6,134},{7,135},{8... | collective-permute-start | bytes 4616 | tf_op jit(solution)/shard_map/ppermute | solution.py:381
  42.1 4.5 %collective-permute-start.5 = (f32[3,128]{1,0:T(4,128)S(1)}, f32[3,128]{1,0:T(4,128)S(1)}, u32[]{:S(2)}, u32[]{:S(2)}) collective-permute-start(f32[3,128]{1,0:T(4,128)S(1)} %add.25), channel_id=1, source_target_pairs={{0,64},{1,65},{2,66},{3,67},{4,68},{5,69},{6,70},{7,71},{8,72},{9,... | collective-permute-start | bytes 4616 | tf_op jit(solution)/shard_map/ppermute | solution.py:381
  46.6 5.5 %collective-permute-start.7 = (f32[3,128]{1,0:T(4,128)S(1)}, f32[3,128]{1,0:T(4,128)S(1)}, u32[]{:S(2)}, u32[]{:S(2)}) collective-permute-start(f32[3,128]{1,0:T(4,128)S(1)} %add.26), channel_id=1, source_target_pairs={{0,16},{1,17},{2,18},{3,19},{4,20},{5,21},{6,22},{7,23},{8,24},{9,... | collective-permute-start | bytes 4616 | tf_op jit(solution)/shard_map/ppermute | solution.py:381
  52.2 3.7 %collective-permute-start.8 = (f32[3,128]{1,0:T(4,128)S(1)}, f32[3,128]{1,0:T(4,128)S(1)}, u32[]{:S(2)}, u32[]{:S(2)}) collective-permute-start(f32[3,128]{1,0:T(4,128)S(1)} %add.27), channel_id=1, source_target_pairs={{0,32},{1,33},{2,34},{3,35},{4,36},{5,37},{6,38},{7,39},{8,40},{9,... | collective-permute-start | bytes 4616 | tf_op jit(solution)/shard_map/ppermute | solution.py:381
  55.8 23.6 %collective-permute-start.9 = (f32[3,128]{1,0:T(4,128)S(1)}, f32[3,128]{1,0:T(4,128)S(1)}, u32[]{:S(2)}, u32[]{:S(2)}) collective-permute-start(f32[3,128]{1,0:T(4,128)S(1)} %add.28), channel_id=1, source_target_pairs={{0,8},{1,9},{2,10},{3,11},{4,12},{5,13},{6,14},{7,15},{8,0},{9,1},... | collective-permute-start | bytes 4616 | tf_op jit(solution)/shard_map/ppermute | solution.py:381
  79.4 3.7 %collective-permute-start.11 = (f32[3,128]{1,0:T(4,128)S(1)}, f32[3,128]{1,0:T(4,128)S(1)}, u32[]{:S(2)}, u32[]{:S(2)}) collective-permute-start(f32[3,128]{1,0:T(4,128)S(1)} %add.29), channel_id=1, source_target_pairs={{0,4},{1,5},{2,6},{3,7},{4,0},{5,1},{6,2},{7,3},{8,12},{9,13},{10,... | collective-permute-start | bytes 4616 | tf_op jit(solution)/shard_map/ppermute | solution.py:381
  83.1 3.6 %collective-permute-start.12 = (f32[3,128]{1,0:T(4,128)S(1)}, f32[3,128]{1,0:T(4,128)S(1)}, u32[]{:S(2)}, u32[]{:S(2)}) collective-permute-start(f32[3,128]{1,0:T(4,128)S(1)} %add.30), channel_id=1, source_target_pairs={{0,1},{1,0},{2,3},{3,2},{4,5},{5,4},{6,7},{7,6},{8,9},{9,8},{10,11... | collective-permute-start | bytes 4616 | tf_op jit(solution)/shard_map/ppermute | solution.py:381
